TPU v7x, 256 devices: a whole 4x4x8 slice. The times are simulated.
256 devices in a mesh: blk: 8 (over y, core), req: 32 (over z, x).
Axes of the slice: x: 4, y: 4, z: 8, core: 2. Of those that a mesh axis runs over, the one named last changes fastest.
Arguments:
- hidden: bfloat16 [12288, 8192], P('req', 'blk'), may hold values from -120 to 120
- input_norm_gain: float32 [8192], replicated, may hold values from 0.1 to 1.9
- query_weight: bfloat16 [8192, 8192], P('req', 'blk')
- keyvalue_weight: bfloat16 [8192, 2048], P('req', 'blk')
- adapter_down: bfloat16 [32, 3, 16, 8192], P('req', None, None, 'blk'), may hold values from -0.0625 to 0.0625
- adapter_up_query: bfloat16 [32, 16, 8192], P('req', None, 'blk'), may hold values from -1.5 to 1.5
- adapter_up_keyvalue: bfloat16 [32, 16, 2048], P('req', None, 'blk'), may hold values from -1.5 to 1.5
- packed_lengths: int32 [32, 4], P('req'), may hold values from 1 to 192, 384 in all within a row
- prompt_adapter: int32 [32, 4], P('req'), may hold values from 0 to 31
Outputs:
- context: bfloat16 [12288, 8192], P('req', 'blk')
- key_cache: bfloat16 [12288, 1024], P('req', 'blk')
- value_cache: bfloat16 [12288, 1024], P('req', 'blk')
Inputs may be any that keep to these rules, and one draw needn't show every extreme that they name: `packed_lengths`: each row sums to 384; the longest prompt of the whole draw has 192 tokens.
All inputs are finite; a program needn't handle non-finite values.
Results may differ from a plain program's by a relative error of at most 0.012.
The roundings to bfloat16 on the way count: a program that leaves them out, or rounds other values in their place, can miss the bound.
Values may be sent and summed in bfloat16 or wider, within the bound.
A program may use at most 128 MiB of HBM per device.

v0:
```python
import math
import jax
import jax.numpy as jnp
from jax import lax
from jax.sharding import PartitionSpec as P

HEAD_WIDTH = 128
QUERY_LOCAL = 8
KEYVALUE_LOCAL = 1
epsilon = 1e-05
adapter_scale = 2.0
rope_base = 10000.0


def apply_rotation(vectors, cosine_table, sine_table):
    half_size = vectors.shape[-1] // 2
    first_half = vectors[..., :half_size]
    second_half = vectors[..., half_size:]
    turned = jnp.concatenate([-second_half, first_half], axis=-1)
    return vectors * cosine_table + turned * sine_table


def layout(lengths, count):
    slot_index = jnp.arange(count, dtype=jnp.int32)
    prompt_ends = jnp.cumsum(lengths)
    prompt_starts = prompt_ends - lengths
    member = (slot_index[:, None] >= prompt_starts[None, :]) & (
        slot_index[:, None] < prompt_ends[None, :]
    )
    position = jnp.sum(jnp.where(member, slot_index[:, None] - prompt_starts[None, :], 0), axis=1)
    owner = jnp.sum((slot_index[:, None] >= prompt_ends[None, :]).astype(jnp.int32), axis=1)
    return (member.astype(jnp.float32), position, owner, slot_index)


def rope_tables(position, head_size):
    frequency = rope_base ** (-(jnp.arange(head_size // 2, dtype=jnp.float32) * 2.0 / head_size))
    angles = position.astype(jnp.float32)[:, None] * frequency[None, :]
    cosine_table = jnp.cos(angles)
    sine_table = jnp.sin(angles)
    return (
        jnp.concatenate([cosine_table, cosine_table], 1)[:, None, :],
        jnp.concatenate([sine_table, sine_table], 1)[:, None, :],
    )


def shards(
    hidden,
    input_norm_gain,
    query_weight,
    keyvalue_weight,
    adapter_down,
    adapter_up_query,
    adapter_up_keyvalue,
    packed_lengths,
    prompt_adapter,
):
    row_number, feature_cols = hidden.shape
    full_width = feature_cols * lax.axis_size("blk")
    offset = lax.axis_index("blk") * feature_cols
    values = hidden.astype(jnp.float32)
    gain_part = lax.dynamic_slice_in_dim(input_norm_gain, offset, feature_cols, 0)
    squares = lax.psum(jnp.sum(values * values, axis=1), "blk")
    factor = lax.rsqrt(squares / full_width + epsilon)
    normed_part = (values * factor[:, None] * gain_part[None, :]).astype(jnp.bfloat16)
    normed = lax.all_gather(normed_part, "blk", axis=1, tiled=True)
    query_cols = query_weight.shape[1]

    def add_rows(weight_piece):
        return jnp.dot(normed, weight_piece, preferred_element_type=jnp.float32)

    query_plain = add_rows(lax.all_gather(query_weight, "req", axis=0, tiled=True))
    base_pair = add_rows(lax.all_gather(keyvalue_weight, "req", axis=0, tiled=True))
    down_all, up_query_all, up_pair_all = (
        lax.all_gather(adapter_down, "req", axis=0, tiled=True),
        lax.all_gather(adapter_up_query, "req", axis=0, tiled=True),
        lax.all_gather(adapter_up_keyvalue, "req", axis=0, tiled=True),
    )
    adapter_count = down_all.shape[0]
    lengths = packed_lengths[0]
    member, position, owner, slot_index = layout(lengths, row_number)
    prompt_count = lengths.shape[0]
    picked_adapter = (
        prompt_adapter[0][:, None] == jnp.arange(adapter_count, dtype=jnp.int32)[None, :]
    ).astype(jnp.bfloat16)
    down_selected = jnp.einsum(
        "pa,ajrd->pjrd", picked_adapter, down_all, preferred_element_type=jnp.float32
    ).astype(jnp.bfloat16)
    rank_size = down_selected.shape[2]
    partial_value = lax.dot_general(
        normed_part,
        down_selected.reshape(prompt_count * 3 * rank_size, feature_cols),
        (((1,), (1,)), ((), ())),
        preferred_element_type=jnp.float32,
    )
    partial_value = partial_value.reshape(row_number, prompt_count, 3, rank_size)
    masked = jnp.sum(partial_value * member[:, :, None, None], axis=1).reshape(
        row_number, 3 * rank_size
    )
    low_rank = lax.psum(masked, "blk").reshape(row_number, 3, rank_size).astype(jnp.bfloat16)
    low_float = low_rank.astype(jnp.float32)

    def spread(column):
        return (
            (member[:, :, None] * low_float[:, None, column, :])
            .astype(jnp.bfloat16)
            .reshape(row_number, prompt_count * rank_size)
        )

    up_query_selected = jnp.einsum(
        "pa,arc->prc", picked_adapter, up_query_all, preferred_element_type=jnp.float32
    ).astype(jnp.bfloat16)
    up_keyvalue_selected = jnp.einsum(
        "pa,arc->prc", picked_adapter, up_pair_all, preferred_element_type=jnp.float32
    ).astype(jnp.bfloat16)
    up_keyvalue_selected = up_keyvalue_selected.reshape(
        prompt_count, rank_size, KEYVALUE_LOCAL, 2, HEAD_WIDTH
    )
    query_update = jnp.dot(
        spread(0),
        up_query_selected.reshape(prompt_count * rank_size, query_cols),
        preferred_element_type=jnp.float32,
    )
    key_update = jnp.dot(
        spread(1),
        up_keyvalue_selected[:, :, :, 0].reshape(
            prompt_count * rank_size, KEYVALUE_LOCAL * HEAD_WIDTH
        ),
        preferred_element_type=jnp.float32,
    )
    value_update = jnp.dot(
        spread(2),
        up_keyvalue_selected[:, :, :, 1].reshape(
            prompt_count * rank_size, KEYVALUE_LOCAL * HEAD_WIDTH
        ),
        preferred_element_type=jnp.float32,
    )
    cosine_table, sine_table = rope_tables(position, HEAD_WIDTH)
    query_complete = (query_plain + adapter_scale * query_update).reshape(
        row_number, QUERY_LOCAL * KEYVALUE_LOCAL, HEAD_WIDTH
    )
    query_states = apply_rotation(query_complete, cosine_table, sine_table).astype(jnp.bfloat16)
    keyvalue_plain = base_pair.reshape(row_number, KEYVALUE_LOCAL, 2, HEAD_WIDTH)
    key_vectors = apply_rotation(
        keyvalue_plain[:, :, 0]
        + adapter_scale * key_update.reshape(row_number, KEYVALUE_LOCAL, HEAD_WIDTH),
        cosine_table,
        sine_table,
    ).astype(jnp.bfloat16)
    value_vectors = (
        keyvalue_plain[:, :, 1]
        + adapter_scale * value_update.reshape(row_number, KEYVALUE_LOCAL, HEAD_WIDTH)
    ).astype(jnp.bfloat16)
    grouped = query_states.reshape(row_number, KEYVALUE_LOCAL, QUERY_LOCAL, HEAD_WIDTH)
    scores = jnp.einsum(
        "tkgc,skc->kgts", grouped, key_vectors, preferred_element_type=jnp.float32
    ) / math.sqrt(HEAD_WIDTH)
    allowed = (owner[:, None] == owner[None, :]) & (slot_index[None, :] <= slot_index[:, None])
    scores = jnp.where(allowed[None, None], scores, -1e30)
    row_max = jnp.max(scores, axis=-1, keepdims=True)
    exponent = jnp.exp(scores - row_max)
    attend = (exponent / jnp.sum(exponent, axis=-1, keepdims=True)).astype(jnp.bfloat16)
    context = jnp.einsum(
        "kgts,skc->tkgc", attend, value_vectors, preferred_element_type=jnp.float32
    ).astype(jnp.bfloat16)
    return (
        context.reshape(row_number, KEYVALUE_LOCAL * QUERY_LOCAL * HEAD_WIDTH),
        key_vectors.reshape(row_number, KEYVALUE_LOCAL * HEAD_WIDTH),
        value_vectors.reshape(row_number, KEYVALUE_LOCAL * HEAD_WIDTH),
    )


def solution(mesh):
    in_specs = (
        P("req", "blk"),
        P(),
        P("req", "blk"),
        P("req", "blk"),
        P("req", None, None, "blk"),
        P("req", None, "blk"),
        P("req", None, "blk"),
        P("req", None),
        P("req", None),
    )
    out_specs = (P("req", "blk"), P("req", "blk"), P("req", "blk"))
    return jax.shard_map(shards, mesh=mesh, in_specs=in_specs, out_specs=out_specs, check_vma=False)
```

profile of v0, /device:TPU:1, one launch (start us, length us, event | category | flops | bytes accessed | tf_op | source)
XLA Modules:
  0.0 463.0 jit_solution(1548275453089813098)
XLA Ops:
  7.2 0.0 copy-start
  7.2 0.0 all-gather.14.cloned.1.call-start
  7.2 0.7 all-gather.14.cloned.1.call-update
  7.9 0.0 all-gather.10.cloned.1.call-start
  8.0 0.7 all-gather.10.cloned.1.call-update
  8.7 0.0 all-gather.8.cloned.1.call-start
  8.7 0.7 all-gather.8.cloned.1.call-update
  9.4 0.0 all-gather.6.cloned.1.call-start
  9.4 0.7 dynamic_slice.3
  10.1 1.4 fusion.7
  11.5 0.0 copy-start.6
  11.5 0.0 copy-start.4
  11.5 15.0 %psum.14 = f32[384]{0:T(512)S(1)} all-reduce(f32[384]{0:T(512)S(1)} %fusion.7), channel_id=1, replica_groups=mesh['blk'=8,'req'=32] {'blk'}, use_global_device_ids=true, to_apply=%region_1.0 | all-reduce | flops 384 | bytes 3072 | tf_op jit(solution)/shard_map/psum | solution.py:62
  26.5 0.0 copy-done
  26.5 0.0 copy-start.5
  26.6 1.1 fusion.9
  27.7 0.0 all-gather.6.cloned.1.call-update
  27.7 0.0 all-gather.12.cloned.1.call-start
  27.8 0.5 all-gather.12.cloned.1.call-update
  28.3 0.0 copy-done.6
  28.3 0.2 reduce-window.4
  28.5 0.0 copy-done.4
  28.5 40.4 %all_gather.21 = bf16[32,16,256]{2,1,0:T(8,128)(2,1)S(1)} all-gather(bf16[1,16,256]{2,1,0:T(8,128)(2,1)S(1)} %copy-done.4), channel_id=1, replica_groups=mesh['blk'=8,'req'=32] {'req'}, dimensions={0}, use_global_device_ids=true | all-gather | bytes 270336 | tf_op jit(solution)/shard_map/all_gather | solution.py:76
  68.9 0.0 copy-done.5
  68.9 0.2 convolution_convert_fusion.1
  69.2 0.1 fusion.54
  69.3 0.1 convert_reduce_fusion
  69.4 0.1 fusion.52
  69.5 0.1 fusion.28
  69.6 0.8 multiply_cosine_fusion
  70.4 16.0 %all-gather.14.cloned.1.call-done = bf16[32,16,1024]{2,1,0:T(8,128)(2,1)} async-done(((bf16[1,16,1024]{2,1,0:T(8,128)(2,1)}), bf16[32,16,1024]{2,1,0:T(8,128)(2,1)}) %all-gather.14.cloned.1.call-update) | async-done | bytes 1048592 | tf_op jit(solution)/shard_map/all_gather | solution.py:75
  86.3 2.4 convolution_convert_fusion
  88.8 0.0 copy-start.1
  88.8 78.0 %all-gather.10.cloned.1.call-done = bf16[32,3,16,1024]{3,2,1,0:T(8,128)(2,1)} async-done(((bf16[1,3,16,1024]{3,2,1,0:T(8,128)(2,1)}), bf16[32,3,16,1024]{3,2,1,0:T(8,128)(2,1)}) %all-gather.10.cloned.1.call-update) | async-done | bytes 3145744 | tf_op jit(solution)/shard_map/all_gather | solution.py:74
  166.8 5.4 %fusion.15 = bf16[4,3,16,1024]{3,0,2,1:T(4,128)(2,1)S(1)} fusion(bf16[32,3,16,1024]{3,2,1,0:T(8,128)(2,1)} %all-gather.10.cloned.1.call-done, s32[4]{0:T(128)S(1)} %bitcast.137), kind=kOutput, calls=%fused_computation.23 | convolution fusion | flops 12779648 | bytes 3538960 | tf_op jit(solution)/shard_map/pa,ajrd->pjrd/dot_general | solution.py:85
  172.1 0.0 copy-done.1
  172.1 0.5 fusion.20
  172.6 26.5 %psum.15 = bf16[384,48]{0,1:T(8,128)(2,1)S(1)} all-reduce(f32[384,48]{0,1:T(8,128)S(1)} %bitcast.132), channel_id=1, replica_groups=mesh['blk'=8,'req'=32] {'blk'}, use_global_device_ids=true, to_apply=%region_4.5 | all-reduce | flops 18432 | bytes 110592 | tf_op jit(solution)/shard_map/psum | solution.py:99
  199.1 0.4 fusion.34
  199.5 49.6 %all-gather.8.cloned.1.call-done = bf16[8192,256]{1,0:T(8,128)(2,1)} async-done(((bf16[256,256]{1,0:T(8,128)(2,1)}), bf16[8192,256]{1,0:T(8,128)(2,1)}) %all-gather.8.cloned.1.call-update) | async-done | bytes 4194320 | tf_op jit(solution)/shard_map/all_gather | solution.py:72
  249.1 46.2 %all-gather.6.cloned.1.call-done = bf16[384,8192]{1,0:T(8,128)(2,1)} async-done(((bf16[384,1024]{1,0:T(8,128)(2,1)}), bf16[384,8192]{1,0:T(8,128)(2,1)}) %all-gather.6.cloned.1.call-update) | async-done | bytes 6291472 | tf_op jit(solution)/shard_map/all_gather | solution.py:65
  295.4 6.4 %fusion.55 = f32[384,256]{0,1:T(8,128)S(1)} fusion(bf16[384,8192]{1,0:T(8,128)(2,1)} %all-gather.6.cloned.1.call-done, bf16[8192,256]{1,0:T(8,128)(2,1)} %all-gather.8.cloned.1.call-done), kind=kOutput, calls=%fused_computation.86 | convolution fusion | flops 1610612736 | bytes 10878976 | tf_op jit(solution)/shard_map/dot_general | solution.py:69
  301.8 0.1 copy.52
  301.9 0.1 copy.50
  302.1 0.2 fusion.21
  302.3 0.0 copy-start.3
  302.3 0.2 fusion.18
  302.5 0.1 fusion.31
  302.6 0.2 fusion.33
  302.9 0.0 copy-start.2
  302.9 134.8 %all-gather.12.cloned.1.call-done = bf16[8192,1024]{1,0:T(8,128)(2,1)} async-done(((bf16[256,1024]{1,0:T(8,128)(2,1)}), bf16[8192,1024]{1,0:T(8,128)(2,1)}) %all-gather.12.cloned.1.call-update) | async-done | bytes 16777232 | tf_op jit(solution)/shard_map/all_gather | solution.py:71
  437.7 12.0 %fusion.11 = f32[384,1024]{1,0:T(8,128)S(1)} fusion(f32[384,1024,1]{1,0,2:T(8,128)S(1)} %fusion.34, bf16[384,8192]{1,0:T(8,128)(2,1)} %all-gather.6.cloned.1.call-done, bf16[8192,1024]{1,0:T(8,128)(2,1)} %all-gather.12.cloned.1.call-done), kind=kOutput, calls=%fused_computation.21 | convolution fusion | flops 6443237376 | bytes 26214400 | tf_op jit(solution)/shard_map/dot_general | solution.py:69
  449.7 0.3 copy.56
  450.0 0.5 slice_negate_fusion
  450.6 0.6 maximum_multiply_fusion
  451.1 0.1 mul.179
  451.2 0.0 copy-done.2
  451.2 1.4 fusion.1
  452.7 1.0 fusion
  453.7 0.0 copy-done.3
  453.7 1.6 fusion.12
  455.3 1.2 copy.43
  (11 shorter events, 0.1 us)
Async XLA Ops:
  7.2 19.4 %copy-start = (bf16[384,1024]{1,0:T(8,128)(2,1)S(1)}, bf16[384,1024]{1,0:T(8,128)(2,1)}, u32[]{:S(2)}) copy-start(bf16[384,1024]{1,0:T(8,128)(2,1)} %param.9) | copy-start | bytes 2359300
  7.2 79.1 %all-gather.14.cloned.1.call-start = ((), (), s32[]{:S(2)}) async-start(), calls=%async_computation.4 | async-start | bytes 1081344 | tf_op jit(solution)/shard_map/all_gather | solution.py:75
  7.9 158.9 %all-gather.10.cloned.1.call-start = ((), (), s32[]{:S(2)}) async-start(), calls=%async_computation.2 | async-start | bytes 3244032 | tf_op jit(solution)/shard_map/all_gather | solution.py:74
  8.7 240.5 %all-gather.8.cloned.1.call-start = ((), (), s32[]{:S(2)}) async-start(), calls=%async_computation.1 | async-start | bytes 4325376 | tf_op jit(solution)/shard_map/all_gather | solution.py:72
  9.4 286.0 %all-gather.6.cloned.1.call-start = ((), (), s32[]{:S(2)}) async-start(), calls=%async_computation | async-start | bytes 7077888 | tf_op jit(solution)/shard_map/all_gather | solution.py:65
  11.5 16.8 %copy-start.6 = (s32[1,4]{1,0:T(1,128)S(1)}, s32[1,4]{1,0:T(1,128)}, u32[]{:S(2)}) copy-start(s32[1,4]{1,0:T(1,128)} %param.16) | copy-start | bytes 52
  11.5 17.0 %copy-start.4 = (bf16[1,16,256]{2,1,0:T(8,128)(2,1)S(1)}, bf16[1,16,256]{2,1,0:T(8,128)(2,1)}, u32[]{:S(2)}) copy-start(bf16[1,16,256]{2,1,0:T(8,128)(2,1)} %param.15) | copy-start | bytes 24580
  26.5 42.4 %copy-start.5 = (s32[1,4]{1,0:T(1,128)S(1)}, s32[1,4]{1,0:T(1,128)}, u32[]{:S(2)}) copy-start(s32[1,4]{1,0:T(1,128)} %param.17) | copy-start | bytes 52
  27.7 410.0 %all-gather.12.cloned.1.call-start = ((), (), s32[]{:S(2)}) async-start(), calls=%async_computation.3 | async-start | bytes 17301504 | tf_op jit(solution)/shard_map/all_gather | solution.py:71
  88.8 83.4 %copy-start.1 = (bf16[384,1024]{1,0:T(8,128)(2,1)S(1)}, bf16[384,1024]{1,0:T(8,128)(2,1)}, u32[]{:S(2)}) copy-start(bf16[384,1024]{1,0:T(8,128)(2,1)} %fusion.9) | copy-start | bytes 2359300
  302.3 151.4 %copy-start.3 = (bf16[384,128]{1,0:T(8,128)(2,1)}, bf16[384,128]{1,0:T(8,128)(2,1)S(1)}, u32[]{:S(2)}) copy-start(bf16[384,128]{1,0:T(8,128)(2,1)S(1)} %fusion.21) | copy-start | bytes 294916
  302.9 148.4 %copy-start.2 = (bf16[384,128]{1,0:T(8,128)(2,1)}, bf16[384,128]{1,0:T(8,128)(2,1)S(1)}, u32[]{:S(2)}) copy-start(bf16[384,128]{1,0:T(8,128)(2,1)S(1)} %get-tuple-element.18) | copy-start | bytes 294916
Sparse Core Ops, SparseCore 0:
  10.6 75.6 all-gather.13
  88.9 77.8 all-gather.9
  169.3 79.7 all-gather.7
  251.4 43.9 all-gather.5
  297.8 139.8 all-gather.11
where the time goes:
time: 463 us
  waiting for transfers between devices  327 us (71%)
  blocking collectives  81.9 us (18%)
  matrix products  30.7 us (7%)
  between operations  14 us (3%)
  other arithmetic  6.18 us (1%)
    all_gather x1, waiting for transfers between devices, shards(): lax.all_gather(query_weight, 'req', axis=0, tiled=True)  135 us
    all_gather x1, waiting for transfers between devices, shards(): lax.all_gather(adapter_down, 'req', axis=0, tiled=True)  78 us
    all_gather x1, waiting for transfers between devices, shards(): lax.all_gather(keyvalue_weight, 'req', axis=0, tiled=True)  49.6 us
    all_gather x1, waiting for transfers between devices, shards(): normed = lax.all_gather(normed_part, 'blk', axis=1, tiled=True)  46.2 us
    all_gather x1, blocking collectives, shards(): lax.all_gather(adapter_up_keyvalue, 'req', axis=0, tiled=True)  40.4 us
    psum x1, blocking collectives, shards(): lax.psum(masked, 'blk').reshape(row_number, 3, rank_size)  26.5 us
    dot_general x2, matrix products, add_rows(): return jnp.dot(normed, weight_piece, preferred_element_type=jnp.float32)  18.4 us
    all_gather x1, waiting for transfers between devices, shards(): lax.all_gather(adapter_up_query, 'req', axis=0, tiled=True)  16 us
  transfers between devices with their start and end apart: 5, of which 5 were waited for; matrix products, arithmetic and copies ran while one was open for 5% of the time, Pallas kernels for 0%

commit v1 on v0

--- a/solution.py
+++ b/solution.py
@@ -1,3 +1,4 @@
+import functools
 import math
 import jax
 import jax.numpy as jnp
@@ -10,6 +11,16 @@
 epsilon = 1e-05
 adapter_scale = 2.0
 rope_base = 10000.0
+
+
+def _compute_inputs(array_here, link_axis):
+    later = lax.axis_size(link_axis)
+    y1 = jnp.stack([array_here] * later, axis=0)
+    h_now = lax.all_to_all(y1, link_axis, 0, 0)
+    return jnp.concatenate(h_now, axis=0)
+
+
+make_links_in = functools.partial(_compute_inputs, link_axis="req")
 
 
 def apply_rotation(vectors, cosine_table, sine_table):
@@ -71,7 +82,7 @@
     query_plain = add_rows(lax.all_gather(query_weight, "req", axis=0, tiled=True))
     base_pair = add_rows(lax.all_gather(keyvalue_weight, "req", axis=0, tiled=True))
     down_all, up_query_all, up_pair_all = (
-        lax.all_gather(adapter_down, "req", axis=0, tiled=True),
+        make_links_in(adapter_down),
         lax.all_gather(adapter_up_query, "req", axis=0, tiled=True),
         lax.all_gather(adapter_up_keyvalue, "req", axis=0, tiled=True),
     )

time: 463 us -> 412 us (0.89)
  waiting for transfers between devices: 327 us -> 188 us
  blocking collectives: 81.9 us -> 156 us
  starting transfers between devices: 0.19 us -> 9.76 us
    all_gather x1 -> x0, waiting for transfers between devices: 78 us -> none  [shards(): lax.all_gather(adapter_down, 'req', axis=0, tiled=True)]
    all_gather x1, blocking collectives: 40.4 us -> 105 us  [shards(): lax.all_gather(adapter_up_keyvalue, 'req', axis=0, tiled=True)]
    all_gather x1, waiting for transfers between devices: 49.6 us -> 5.45 us  [shards(): lax.all_gather(keyvalue_weight, 'req', axis=0, tiled=True)]
    all_gather x1, waiting for transfers between devices: 16 us -> 0.01 us  [shards(): lax.all_gather(adapter_up_query, 'req', axis=0, tiled=True)]
    all_to_all x0 -> x1, starting transfers between devices: none -> 9.61 us  [_compute_inputs(): h_now = lax.all_to_all(y1, link_axis, 0, 0)]
    psum x1, blocking collectives: 26.5 us -> 35.5 us  [shards(): lax.psum(masked, 'blk').reshape(row_number, 3, rank_size)]
  transfers between devices with their start and end apart: 5 -> 5, of which waited for: 5 -> 3; matrix products, arithmetic and copies ran while one was open for 5% -> 6% of each run, Pallas kernels for 0% -> 0%
where the time goes in v1:
time: 412 us; the launch traced here: 411 us
  waiting for transfers between devices  188 us (46%)
  blocking collectives  156 us (38%)
  matrix products  30.4 us (7%)
  between operations  14 us (3%)
  starting transfers between devices  9.76 us (2%)
  other arithmetic  8 us (2%)
  local copies, waits for them, and re-layouts  4.89 us (1%)
    all_gather x1, waiting for transfers between devices, shards(): lax.all_gather(query_weight, 'req', axis=0, tiled=True)  135 us
    all_gather x1, blocking collectives, shards(): lax.all_gather(adapter_up_keyvalue, 'req', axis=0, tiled=True)  105 us
    all_gather x1, waiting for transfers between devices, shards(): normed = lax.all_gather(normed_part, 'blk', axis=1, tiled=True)  46.2 us
    psum x1, blocking collectives, shards(): lax.psum(masked, 'blk').reshape(row_number, 3, rank_size)  35.5 us
    dot_general x2, matrix products, add_rows(): return jnp.dot(normed, weight_piece, preferred_element_type=jnp.float32)  18.4 us
    psum x1, blocking collectives, shards(): squares = lax.psum(jnp.sum(values * values, axis=1), 'blk')  15 us
    all_to_all x1, starting transfers between devices, _compute_inputs(): h_now = lax.all_to_all(y1, link_axis, 0, 0)  9.61 us
  transfers between devices with their start and end apart: 5, of which 3 were waited for; matrix products, arithmetic and copies ran while one was open for 6% of the time, Pallas kernels for 0%

profile of v1, /device:TPU:1, one launch (start us, length us, event | category | flops | bytes accessed | tf_op | source)
XLA Modules:
  0.0 411.2 jit_solution(17709250622139892717)
XLA Ops:
  7.2 0.0 copy-start.3
  7.2 0.0 all-gather.11.cloned.1.call-start
  7.2 0.7 all-gather.11.cloned.1.call-update
  7.9 0.0 all-gather.7.cloned.1.call-start
  8.0 0.7 all-gather.7.cloned.1.call-update
  8.7 0.0 all-gather.5.cloned.1.call-start
  8.7 0.7 dynamic_slice.3
  9.4 1.4 fusion.8
  10.8 15.0 %psum.14 = f32[384]{0:T(512)S(1)} all-reduce(f32[384]{0:T(512)S(1)} %fusion.8), channel_id=1, replica_groups=mesh['blk'=8,'req'=32] {'blk'}, use_global_device_ids=true, to_apply=%region_1.0 | all-reduce | flops 384 | bytes 3072 | tf_op jit(solution)/shard_map/psum | solution.py:73
  25.8 2.3 fusion.10
  28.1 0.0 all-gather.5.cloned.1.call-update
  28.1 0.0 all-gather.9.cloned.1.call-start
  28.1 0.5 all-gather.9.cloned.1.call-update
  28.7 0.0 copy-done.3
  28.7 2.1 stack.2
  30.8 0.0 copy-start.7
  30.8 0.0 copy-start.5
  30.8 0.0 copy-start.6
  30.8 9.6 %all-to-all-start = ((bf16[32,1,3,16,1024]{4,3,2,1,0:T(8,128)(2,1)}), bf16[32,1,3,16,1024]{4,3,2,1,0:T(8,128)(2,1)S(1)}, u32[]{:S(2)}, u32[]{:S(2)}) async-start(bf16[32,1,3,16,1024]{4,3,2,1,0:T(8,128)(2,1)} %stack.2), calls=%async_computation | async-start | bytes 6291456 | tf_op jit(solution)/shard_map/all_to_all | solution.py:19
  40.4 0.0 copy-done.7
  40.4 0.2 reduce-window.4
  40.6 0.0 copy-done.5
  40.6 105.3 %all_gather.17 = bf16[32,16,256]{2,1,0:T(8,128)(2,1)S(1)} all-gather(bf16[1,16,256]{2,1,0:T(8,128)(2,1)S(1)} %copy-done.5), channel_id=1, replica_groups=mesh['blk'=8,'req'=32] {'req'}, dimensions={0}, use_global_device_ids=true | all-gather | bytes 270336 | tf_op jit(solution)/shard_map/all_gather | solution.py:87
  145.9 0.0 copy-done.6
  145.9 0.2 convolution_convert_fusion.1
  146.2 0.1 fusion.55
  146.3 0.1 convert_reduce_fusion
  146.4 0.1 fusion.53
  146.5 0.1 fusion.29
  146.6 1.4 multiply_cosine_fusion
  148.0 0.0 all-gather.11.cloned.1.call-done
  148.0 3.1 convolution_convert_fusion
  151.1 0.0 all-to-all-done
  151.1 0.0 copy-start
  151.1 3.5 fusion.16
  154.6 0.0 copy-done
  154.6 0.5 fusion.21
  155.1 35.5 %psum.15 = bf16[384,48]{0,1:T(8,128)(2,1)S(1)} all-reduce(f32[384,48]{0,1:T(8,128)S(1)} %bitcast.139), channel_id=1, replica_groups=mesh['blk'=8,'req'=32] {'blk'}, use_global_device_ids=true, to_apply=%region_4.5 | all-reduce | flops 18432 | bytes 110592 | tf_op jit(solution)/shard_map/psum | solution.py:110
  190.6 1.3 fusion.35
  191.9 5.4 %all-gather.7.cloned.1.call-done = bf16[8192,256]{1,0:T(8,128)(2,1)} async-done(((bf16[256,256]{1,0:T(8,128)(2,1)}), bf16[8192,256]{1,0:T(8,128)(2,1)}) %all-gather.7.cloned.1.call-update) | async-done | bytes 4194320 | tf_op jit(solution)/shard_map/all_gather | solution.py:83
  197.4 46.2 %all-gather.5.cloned.1.call-done = bf16[384,8192]{1,0:T(8,128)(2,1)} async-done(((bf16[384,1024]{1,0:T(8,128)(2,1)}), bf16[384,8192]{1,0:T(8,128)(2,1)}) %all-gather.5.cloned.1.call-update) | async-done | bytes 6291472 | tf_op jit(solution)/shard_map/all_gather | solution.py:76
  243.5 6.4 %fusion.56 = f32[384,256]{0,1:T(8,128)S(1)} fusion(bf16[384,8192]{1,0:T(8,128)(2,1)} %all-gather.5.cloned.1.call-done, bf16[8192,256]{1,0:T(8,128)(2,1)} %all-gather.7.cloned.1.call-done), kind=kOutput, calls=%fused_computation.87 | convolution fusion | flops 1610612736 | bytes 10878976 | tf_op jit(solution)/shard_map/dot_general | solution.py:80
  249.9 0.0 copy-start.1
  250.0 0.1 copy.65
  250.1 0.1 copy.63
  250.2 0.2 fusion.22
  250.5 0.0 copy-start.4
  250.5 0.2 fusion.19
  250.7 0.1 fusion.32
  250.8 0.0 copy-done.1
  250.8 0.2 fusion.34
  251.1 0.0 copy-start.2
  251.1 134.8 %all-gather.9.cloned.1.call-done = bf16[8192,1024]{1,0:T(8,128)(2,1)} async-done(((bf16[256,1024]{1,0:T(8,128)(2,1)}), bf16[8192,1024]{1,0:T(8,128)(2,1)}) %all-gather.9.cloned.1.call-update) | async-done | bytes 16777232 | tf_op jit(solution)/shard_map/all_gather | solution.py:82
  385.8 12.0 %fusion.12 = f32[384,1024]{1,0:T(8,128)S(1)} fusion(f32[384,1024,1]{1,0,2:T(8,128)S(1)} %fusion.35, bf16[384,8192]{1,0:T(8,128)(2,1)} %all-gather.5.cloned.1.call-done, bf16[8192,1024]{1,0:T(8,128)(2,1)} %all-gather.9.cloned.1.call-done), kind=kOutput, calls=%fused_computation.22 | convolution fusion | flops 6443237376 | bytes 26214400 | tf_op jit(solution)/shard_map/dot_general | solution.py:80
  397.9 0.3 copy.69
  398.2 0.5 slice_negate_fusion
  398.7 0.6 maximum_multiply_fusion
  399.3 0.1 mul.179
  399.4 0.0 copy-done.2
  399.4 1.4 fusion.1
  400.8 1.0 fusion
  401.9 0.0 copy-done.4
  401.9 1.6 fusion.13
  403.5 1.2 copy.56
  (11 shorter events, 0.1 us)
Async XLA Ops:
  7.2 21.5 %copy-start.3 = (bf16[1,3,16,1024]{3,2,1,0:T(8,128)(2,1)S(1)}, bf16[1,3,16,1024]{3,2,1,0:T(8,128)(2,1)}, u32[]{:S(2)}) copy-start(bf16[1,3,16,1024]{3,2,1,0:T(8,128)(2,1)} %param.13) | copy-start | bytes 294916
  7.2 140.9 %all-gather.11.cloned.1.call-start = ((), (), s32[]{:S(2)}) async-start(), calls=%async_computation.4 | async-start | bytes 1081344 | tf_op jit(solution)/shard_map/all_gather | solution.py:86
  7.9 189.5 %all-gather.7.cloned.1.call-start = ((), (), s32[]{:S(2)}) async-start(), calls=%async_computation.2 | async-start | bytes 4325376 | tf_op jit(solution)/shard_map/all_gather | solution.py:83
  8.7 234.9 %all-gather.5.cloned.1.call-start = ((), (), s32[]{:S(2)}) async-start(), calls=%async_computation.1 | async-start | bytes 7077888 | tf_op jit(solution)/shard_map/all_gather | solution.py:76
  28.1 357.8 %all-gather.9.cloned.1.call-start = ((), (), s32[]{:S(2)}) async-start(), calls=%async_computation.3 | async-start | bytes 17301504 | tf_op jit(solution)/shard_map/all_gather | solution.py:82
  30.8 9.6 %copy-start.7 = (s32[1,4]{1,0:T(1,128)S(1)}, s32[1,4]{1,0:T(1,128)}, u32[]{:S(2)}) copy-start(s32[1,4]{1,0:T(1,128)} %param.16) | copy-start | bytes 52
  30.8 9.8 %copy-start.5 = (bf16[1,16,256]{2,1,0:T(8,128)(2,1)S(1)}, bf16[1,16,256]{2,1,0:T(8,128)(2,1)}, u32[]{:S(2)}) copy-start(bf16[1,16,256]{2,1,0:T(8,128)(2,1)} %param.15) | copy-start | bytes 24580
  30.8 115.1 %copy-start.6 = (s32[1,4]{1,0:T(1,128)S(1)}, s32[1,4]{1,0:T(1,128)}, u32[]{:S(2)}) copy-start(s32[1,4]{1,0:T(1,128)} %param.17) | copy-start | bytes 52
  30.8 120.3 %all-to-all-start = ((bf16[32,1,3,16,1024]{4,3,2,1,0:T(8,128)(2,1)}), bf16[32,1,3,16,1024]{4,3,2,1,0:T(8,128)(2,1)S(1)}, u32[]{:S(2)}, u32[]{:S(2)}) async-start(bf16[32,1,3,16,1024]{4,3,2,1,0:T(8,128)(2,1)} %stack.2), calls=%async_computation | async-start | bytes 6291456 | tf_op jit(solution)/shard_map/all_to_all | solution.py:19
  151.1 3.5 copy-start
  249.9 0.9 copy-start.1
  250.5 151.4 %copy-start.4 = (bf16[384,128]{1,0:T(8,128)(2,1)}, bf16[384,128]{1,0:T(8,128)(2,1)S(1)}, u32[]{:S(2)}) copy-start(bf16[384,128]{1,0:T(8,128)(2,1)S(1)} %fusion.22) | copy-start | bytes 294916
  251.1 148.3 %copy-start.2 = (bf16[384,128]{1,0:T(8,128)(2,1)}, bf16[384,128]{1,0:T(8,128)(2,1)S(1)}, u32[]{:S(2)}) copy-start(bf16[384,128]{1,0:T(8,128)(2,1)S(1)} %get-tuple-element.21) | copy-start | bytes 294916
Sparse Core Ops, SparseCore 0:
  10.6 92.9 all-gather.10
  106.1 91.1 all-gather.6
  199.8 43.7 all-gather.4
  246.0 139.8 all-gather.8
